TPU v7x, 256 devices: a whole 4x4x8 slice. The times are simulated.
256 devices in a mesh: replica: 32 (over z_hi, y, core), shard: 8 (over x, z_lo).
Axes of the slice: x: 4, y: 4, z: 8 (z_hi: 4, z_lo: 2; z = z_hi * 2 + z_lo), core: 2. Of those that a mesh axis runs over, the one named last changes fastest.
Arguments:
- weight: bfloat16 [256, 8192], P(None, 'shard'), may hold values from -6 to 6
- momentum: float32 [32, 256, 8192], P('replica', None, 'shard'), may hold values from -6 to 6
- grad: bfloat16 [32, 256, 8192], P('replica', None, 'shard'), may hold values from -6 to 6
- positions: int32 [32, 4, 128, 32], P('replica', None, 'shard'), may hold values from 0 to 4095, as said below
Outputs:
- kept_state: float32 [32, 256, 8192], P('replica', None, 'shard')
- direction: bfloat16 [256, 8192], P(None, 'shard')
- new_weight: bfloat16 [256, 8192], replicated
Inputs may be any that keep to these rules, and one draw needn't show every extreme that they name: The 32 positions of one block on one replica are distinct; replicas choose independently.
All inputs are finite; a program needn't handle non-finite values.
Results may differ from a plain program's by a relative error of at most 0.001.
Values may be sent and summed in bfloat16 or wider, within the bound.
No kernel may reach another device: no remote copies, remote signals or barrier semaphores. Data moves between devices by JAX's collectives and lax.ppermute only.
A program may use at most 64 MiB of HBM per device.

v0:
```python
import math
import jax
import jax.numpy as jnp
from jax import lax
from jax.sharding import Mesh
from jax.sharding import PartitionSpec as P

GROUP = 64
REPLICA = ("replica_0", "replica_1", "replica_2")
beta_decay = 0.9
step_rate = 0.02


def padded_to(lines, size):
    spare = -len(lines) % size
    return jnp.pad(lines, [(0, spare)] + [(0, 0)] * (lines.ndim - 1))


def copy_for_each(array, axis):
    copies = jnp.broadcast_to(array, (lax.axis_size(axis), *array.shape))
    return lax.all_to_all(copies, axis, split_axis=0, concat_axis=0, tiled=True)


def laid_out(blocks, dim):
    blocks = jnp.moveaxis(blocks, 0, dim)
    shape = blocks.shape
    return blocks.reshape(*shape[:dim], shape[dim] * shape[dim + 1], *shape[dim + 2 :])


def whole_of(array, axes, dim):
    far, near = axes
    blocks = copy_for_each(copy_for_each(array, far), near)
    return laid_out(blocks.swapaxes(0, 1).reshape(-1, *array.shape), dim)


def in_blocks(array, dim, size):
    before, after = (array.shape[:dim], array.shape[dim + 1 :])
    return jnp.moveaxis(array.reshape(*before, size, -1, *after), dim, 0)


def sent_and_summed(array, axis, dim):
    size = lax.axis_size(axis)
    blocks = lax.all_to_all(in_blocks(array, dim, size), axis, 0, 0, tiled=True)
    return jnp.sum(blocks, axis=0)


def sum_in_two_steps(array, axes, dim):
    far, near = axes
    blocks = in_blocks(array, dim, lax.axis_size(far))
    nearer = sent_and_summed(blocks, near, dim + 1)
    arrived = lax.all_to_all(nearer, far, split_axis=0, concat_axis=0, tiled=True)
    return arrived.sum(axis=0)


def sum_by_parts(array, axes):
    lines = array.reshape(-1, array.shape[-1])
    padded = padded_to(lines, lax.axis_size(axes[0]) * lax.axis_size(axes[1]))
    whole = whole_of(sum_in_two_steps(padded, axes, 0), axes, 0)
    return lax.slice_in_dim(whole, 0, len(lines)).reshape(array.shape)


def dct_basis():
    freq = jnp.arange(GROUP, dtype=jnp.float32)[:, None]
    cells = jnp.arange(GROUP, dtype=jnp.float32)[None, :]
    scales = jnp.where(freq == 0, math.sqrt(1.0 / GROUP), math.sqrt(2.0 / GROUP))
    return scales * jnp.cos(math.pi * (2.0 * cells + 1.0) * freq / (2.0 * GROUP))


def basis_rows(index, basis_table):
    one_hot = (index[..., None] == jnp.arange(GROUP, dtype=jnp.int32)).astype(jnp.float32)
    return jnp.einsum("xyka,ai->xyki", one_hot, basis_table, precision=lax.Precision.HIGHEST)


def extract(field, pos_table, basis_table):
    row_blocks, col_blocks = (pos_table.shape[0], pos_table.shape[1])
    left_rows = basis_rows(pos_table // GROUP, basis_table)
    right_rows = basis_rows(pos_table % GROUP, basis_table)
    block_view = field.reshape(row_blocks, GROUP, col_blocks, GROUP)
    inner_prod = jnp.einsum(
        "xyki,xiyj->xykj", left_rows, block_view, precision=lax.Precision.HIGHEST
    )
    return jnp.sum(inner_prod * right_rows, axis=-1)


def expand(values, pos_table, basis_table):
    row_blocks, col_blocks = (pos_table.shape[0], pos_table.shape[1])
    left_rows = basis_rows(pos_table // GROUP, basis_table)
    right_rows = basis_rows(pos_table % GROUP, basis_table)
    dense = jnp.einsum(
        "xyki,xyk,xykj->xiyj", left_rows, values, right_rows, precision=lax.Precision.HIGHEST
    )
    return dense.reshape(row_blocks * GROUP, col_blocks * GROUP)


def fill_grid(values, pos_table):
    row_blocks, col_blocks = (pos_table.shape[0], pos_table.shape[1])
    row_index = jnp.arange(row_blocks, dtype=jnp.int32)[:, None, None]
    col_index = jnp.arange(col_blocks, dtype=jnp.int32)[None, :, None]
    flat = jnp.zeros((row_blocks, col_blocks, GROUP * GROUP), jnp.float32)
    return flat.at[row_index, col_index, pos_table].add(values)


def decode(grid, basis_table):
    row_blocks, col_blocks = (grid.shape[0], grid.shape[1])
    square = grid.reshape(row_blocks, col_blocks, GROUP, GROUP)
    dense = jnp.einsum(
        "ai,xyab,bj->xiyj", basis_table, square, basis_table, precision=lax.Precision.HIGHEST
    )
    return dense.reshape(row_blocks * GROUP, col_blocks * GROUP)


def per_device(weight, momentum, grad, positions):
    basis_table = dct_basis()
    own_pos = positions[0]
    moved = beta_decay * momentum[0] + grad[0].astype(jnp.float32)
    picked = extract(moved, own_pos, basis_table)
    kept_state = moved - expand(picked, own_pos, basis_table)
    summed = sum_by_parts(fill_grid(picked, own_pos), (("replica_0", "replica_1"), "replica_2"))
    smooth = jnp.tanh(decode(summed, basis_table))
    updated = (weight.astype(jnp.float32) - step_rate * smooth).astype(jnp.bfloat16)
    new_weight = lax.all_gather(updated, "shard", axis=1, tiled=True)
    direction = smooth.astype(jnp.bfloat16)
    return (kept_state[None], direction, new_weight)


def solution(mesh):
    split = Mesh(
        mesh.devices.reshape(4, 4, 2, mesh.shape["shard"]),
        ("replica_0", "replica_1", "replica_2", "shard"),
    )
    in_specs = (
        P(None, "shard"),
        P(REPLICA, None, "shard"),
        P(REPLICA, None, "shard"),
        P(REPLICA, None, "shard", None),
    )
    out_specs = (P(REPLICA, None, "shard"), P(None, "shard"), P())
    return jax.shard_map(
        per_device, mesh=split, in_specs=in_specs, out_specs=out_specs, check_vma=False
    )
```

profile of v0, /device:TPU:1, one launch (start us, length us, event | category | flops | bytes accessed | tf_op | source)
XLA Modules:
  0.0 219.3 jit_solution(12417028372073017833)
XLA Ops:
  7.2 0.9 add_select_fusion
  8.2 0.8 compare_select_fusion
  8.9 0.8 fusion.10
  9.7 0.8 fusion.11
  10.7 1.9 add.62
  12.8 4.2 %fusion.5 = f32[4,16,32]{2,1,0:T(8,128)S(1)} fusion(f32[4,16,32,64]{3,2,1,0:T(8,128)S(1)} %fusion.11, f32[4,16,32,64]{3,2,1,0:T(8,128)S(1)} %fusion.10, f32[4,64,16,64]{3,2,1,0:T(8,128)} %add.62), kind=kOutput, calls=%fused_computation.7 | convolution fusion | flops 100923392 | bytes 2105344 | tf_op jit(solution)/shard_map/xyki,xiyj->xykj/dot_general | solution.py:79
  17.1 12.2 %scatter_custom_fusion = f32[262144]{0:T(1024)} fusion(s32[2048]{0:T(1024)S(1)} %reshape.127, f32[2048]{0:T(1024)S(1)} %reshape.129, f32[]{:T(128)} %constant.54.clone.1), kind=kCustom, calls=%fused_computation.16 | custom fusion | flops 2048 | bytes 1048580
  29.3 2.7 %reshape_reshape.3 = f32[16,2,2,4096]{3,2,1,0:T(2,128)} reshape(f32[262144]{0:T(1024)} %scatter_custom_fusion) | data formatting | bytes 2097152 | tf_op jit(solution)/shard_map/reshape;reshape | solution.py:38
  32.1 1.3 copy.37
  33.4 8.2 %all_to_all.20 = f32[2,16,2,4096]{3,2,1,0:T(2,128)} all-to-all(f32[2,16,2,4096]{3,2,1,0:T(2,128)S(1)} %copy.37), channel_id=1, replica_groups=mesh['replica_0'=4,'replica_1'=4,'replica_2'=2,'shard'=8] {'replica_2'}, dimensions={0} | all-to-all | bytes 2097152 | tf_op jit(solution)/shard_map/all_to_all | solution.py:43
  41.6 2.9 %reduce_sum.28 = f32[16,2,4096]{2,1,0:T(2,128)} reduce(f32[2,16,2,4096]{3,2,1,0:T(2,128)} %all_to_all.20, f32[]{:T(128)} %constant.54.clone.1), dimensions={0}, to_apply=%region_2.3 | reduce | flops 131072 | bytes 1572868 | tf_op jit(solution)/shard_map/reduce_sum | solution.py:44
  44.5 24.6 %all_to_all.21 = f32[16,2,4096]{2,1,0:T(2,128)} all-to-all(f32[16,2,4096]{2,1,0:T(2,128)} %reduce_sum.28), channel_id=1, replica_groups=mesh['replica_0'=4,'replica_1'=4,'replica_2'=2,'shard'=8] {'replica_0','..., dimensions={0} | all-to-all | bytes 1048576 | tf_op jit(solution)/shard_map/all_to_all | solution.py:51
  69.1 1.2 reduce_sum.29
  70.3 0.2 broadcast_in_dim.23
  70.5 20.8 %all_to_all.22 = f32[16,2,4096]{2,1,0:T(2,128)S(1)} all-to-all(f32[16,2,4096]{2,1,0:T(2,128)S(1)} %broadcast_in_dim.23), channel_id=1, replica_groups=mesh['replica_0'=4,'replica_1'=4,'replica_2'=2,'shard'=8] {'replica_0','..., dimensions={0} | all-to-all | bytes 1048576 | tf_op jit(solution)/shard_map/all_to_all | solution.py:21
  91.3 0.6 broadcast_in_dim.24
  91.9 7.8 %all_to_all.23 = f32[2,16,2,4096]{3,2,1,0:T(2,128)S(1)} all-to-all(f32[2,16,2,4096]{3,2,1,0:T(2,128)S(1)} %broadcast_in_dim.24), channel_id=1, replica_groups=mesh['replica_0'=4,'replica_1'=4,'replica_2'=2,'shard'=8] {'replica_2'}, dimensions={0} | all-to-all | bytes 2097152 | tf_op jit(solution)/shard_map/all_to_all | solution.py:21
  99.7 1.0 copy.39
  100.8 3.2 %reshape_reshape_reshape_reshape.3 = f32[4,16,64,64]{3,2,1,0:T(8,128)} reshape(f32[16,2,2,4096]{3,2,1,0:T(2,128)} %copy.39) | data formatting | bytes 2097152 | tf_op jit(solution)/shard_map/reshape;reshape;reshape;reshape | solution.py:105
  103.9 3.6 %fusion.19 = f32[4,16,64,64]{2,3,1,0:T(8,128)S(1)} fusion(f32[4,16,64,64]{3,2,1,0:T(8,128)} %reshape_reshape_reshape_reshape.3, f32[64]{0:T(128)S(1)} %get-tuple-element.8, f32[64]{0:T(128)S(1)} %get-tuple-element.7), kind=kOutput, calls=%fused_computation.32 | convolution fusion | flops 201338880 | bytes 2097664 | tf_op jit(solution)/shard_map/ai,xyab,bj->xiyj/dot_general | solution.py:106
  107.6 3.0 %multiply_bitcast_fusion = (f32[4,64,16,64]{3,1,2,0:T(8,128)S(1)}, bf16[4,64,16,64]{3,1,2,0:T(8,128)(2,1)}) fusion(f32[4,16,64,64]{2,3,1,0:T(8,128)S(1)} %fusion.19, f32[64]{0:T(128)S(1)} %get-tuple-element.8, f32[64]{0:T(128)S(1)} %get-tuple-element.7), kind=kOutput, calls=%fused_computation.3 | convolution fusion | flops 201863168 | bytes 2621952 | tf_op jit(solution)/shard_map/ai,xyab,bj->xiyj/dot_general | solution.py:106
  110.5 2.5 %copy.43 = f32[4,64,16,64]{3,2,1,0:T(8,128)} copy(f32[4,64,16,64]{3,1,2,0:T(8,128)S(1)} %get-tuple-element.3) | data formatting | bytes 2097152 | tf_op jit(solution)/shard_map/mul | solution.py:120
  113.1 2.7 %mul.124 = f32[256,1024]{1,0:T(8,128)} reshape(f32[4,64,16,64]{3,2,1,0:T(8,128)} %copy.43) | data formatting | bytes 2097152 | tf_op jit(solution)/shard_map/mul | solution.py:120
  115.8 2.3 %subtract_convert_fusion = bf16[256,1024]{1,0:T(8,128)(2,1)} fusion(f32[256,1024]{1,0:T(8,128)} %mul.124, bf16[256,1024]{1,0:T(8,128)(2,1)} %param.4), kind=kLoop, calls=%fused_computation.9 | loop fusion | flops 786432 | bytes 2097152 | tf_op jit(solution)/shard_map/convert_element_type | solution.py:120
  118.2 5.1 %convolution_bitcast_fusion = f32[4,64,16,64]{1,3,2,0:T(8,128)} fusion(f32[4,16,32,64]{3,2,1,0:T(8,128)S(1)} %fusion.10, f32[4,16,32,64]{3,2,1,0:T(8,128)S(1)} %fusion.11, f32[4,16,32]{2,1,0:T(8,128)S(1)} %fusion.5), kind=kOutput, calls=%fused_computation.5 | convolution fusion | flops 100794368 | bytes 2105344 | tf_op jit(solution)/shard_map/xyki,xyk,xykj->xiyj/dot_general | solution.py:89
  123.2 2.5 %copy.36 = f32[4,64,16,64]{3,2,1,0:T(8,128)S(1)} copy(f32[4,64,16,64]{1,3,2,0:T(8,128)} %convolution_bitcast_fusion) | data formatting | bytes 2097152 | tf_op jit(solution)/shard_map/xyki,xyk,xykj->xiyj/transpose | solution.py:89
  125.7 1.5 reshape.121
  127.3 2.5 %sub.16 = f32[1,256,1024]{2,1,0:T(8,128)} subtract(f32[1,256,1024]{2,1,0:T(8,128)S(1)} %convert_add_fusion, f32[1,256,1024]{2,1,0:T(8,128)} %reshape.121) | non-fusion elementwise | flops 262144 | bytes 3145728 | tf_op jit(solution)/shard_map/sub | solution.py:117
  129.7 0.7 copy.42
  130.4 1.5 convert_element_type.28
  131.9 75.9 %all-gather.2.cloned.1.call-done = bf16[256,8192]{1,0:T(8,128)(2,1)} async-done(((bf16[256,1024]{1,0:T(8,128)(2,1)}), bf16[256,8192]{1,0:T(8,128)(2,1)}) %all-gather.2.cloned.1.call-update) | async-done | bytes 4194320 | tf_op jit(solution)/shard_map/all_gather | solution.py:121
  207.9 4.6 %copy.55 = bf16[256,8192]{1,0:T(8,128)(2,1)} copy(bf16[256,8192]{1,0:T(8,128)(2,1)} %all-gather.2.cloned.1.call-done) | data formatting | bytes 8388608
  (21 shorter events, 0.6 us)
Async XLA Ops:
  7.2 200.7 %all-gather.2.cloned.1.call-start = ((), (), s32[]{:S(2)}) async-start(), calls=%async_computation.4 | async-start | bytes 4718592 | tf_op jit(solution)/shard_map/all_gather | solution.py:121
  7.2 3.3 %copy-start.1 = (f32[1,256,1024]{2,1,0:T(8,128)S(1)}, f32[1,256,1024]{2,1,0:T(8,128)}, u32[]{:S(2)}) copy-start(f32[1,256,1024]{2,1,0:T(8,128)} %param.5) | copy-start | bytes 3145732
  7.2 3.3 %copy-start.2 = (bf16[1,256,1024]{2,1,0:T(8,128)(2,1)S(1)}, bf16[1,256,1024]{2,1,0:T(8,128)(2,1)}, u32[]{:S(2)}) copy-start(bf16[1,256,1024]{2,1,0:T(8,128)(2,1)} %param.6) | copy-start | bytes 1572868
  10.7 1.9 copy-start.3
  10.7 2.0 copy-start.4
  127.3 2.5 %copy-start = (bf16[4,64,16,64]{3,1,2,0:T(8,128)(2,1)S(1)}, bf16[4,64,16,64]{3,1,2,0:T(8,128)(2,1)}, u32[]{:S(2)}) copy-start(bf16[4,64,16,64]{3,1,2,0:T(8,128)(2,1)} %get-tuple-element.4) | copy-start | bytes 1572868
Sparse Core Ops, SparseCore 0:
  118.3 89.5 all-gather.1
where the time goes:
time: 220 us; the launch traced here: 219 us
  waiting for transfers between devices  76 us (35%)
  blocking collectives  61.4 us (28%)
  local copies, waits for them, and re-layouts  27.2 us (12%)
  other arithmetic  23.1 us (10%)
  matrix products  17.4 us (8%)
  between operations  14.2 us (6%)
    all_gather x1, waiting for transfers between devices, per_device(): new_weight = lax.all_gather(updated, 'shard', axis=1, tiled=True)  75.9 us
    all_to_all x2, blocking collectives, copy_for_each(): return lax.all_to_all(copies, axis, split_axis=0, concat_axis=0, tiled=True)  28.6 us
    all_to_all x1, blocking collectives, sum_in_two_steps(): lax.all_to_all(nearer, far, split_axis=0, concat_axis=0, tiled=True)  24.6 us
    unnamed x4, other arithmetic  12.4 us
    all_to_all x1, blocking collectives, sent_and_summed(): blocks = lax.all_to_all(in_blocks(array, dim, size), axis, 0, 0, tiled=True)  8.23 us
    dot_general x2, matrix products, decode(): jnp.einsum('ai,xyab,bj->xiyj', basis_table, square, basis_table, precisio...  6.6 us
    mul x2, local copies, waits for them, and re-layouts, per_device(): step_rate * smooth  5.27 us
    dot_general x1, matrix products, expand(): jnp.einsum('xyki,xyk,xykj->xiyj', left_rows, values, right_rows, precisio...  5.07 us
  transfers between devices with their start and end apart: 1, of which 1 were waited for; matrix products, arithmetic and copies ran while one was open for 6% of the time, Pallas kernels for 0%

commit v1 on v0

--- a/solution.py
+++ b/solution.py
@@ -118,7 +118,9 @@
     summed = sum_by_parts(fill_grid(picked, own_pos), (("replica_0", "replica_1"), "replica_2"))
     smooth = jnp.tanh(decode(summed, basis_table))
     updated = (weight.astype(jnp.float32) - step_rate * smooth).astype(jnp.bfloat16)
-    new_weight = lax.all_gather(updated, "shard", axis=1, tiled=True)
+    new_weight = jnp.concatenate(
+        lax.all_to_all(jnp.stack([updated] * lax.axis_size("shard")), "shard", 0, 0), axis=1
+    )
     direction = smooth.astype(jnp.bfloat16)
     return (kept_state[None], direction, new_weight)
 

time: 220 us -> 183 us (0.83)
  waiting for transfers between devices: 76 us -> 35.2 us
  between operations: 14.2 us -> 0.79 us
  local copies, waits for them, and re-layouts: 27.2 us -> 39.3 us
  starting transfers between devices: 0.04 us -> 5.51 us
    all_gather x1 -> x0, waiting for transfers between devices: 75.9 us -> none  [per_device(): new_weight = lax.all_gather(updated, 'shard', axis=1, tiled=True)]
    all_to_all x0 -> x1, waiting for transfers between devices: none -> 35.2 us  [per_device(): lax.all_to_all(jnp.stack([updated] * lax.axis_size('shard')), 'shard', 0, 0)]
    all_to_all x0 -> x1, local copies, waits for them, and re-layouts: none -> 6.45 us  [per_device(): lax.all_to_all(jnp.stack([updated] * lax.axis_size('shard')), 'shard', 0, 0)]
    all_to_all x0 -> x1, starting transfers between devices: none -> 5.51 us  [per_device(): lax.all_to_all(jnp.stack([updated] * lax.axis_size('shard')), 'shard', 0, 0)]
    another operation x0 -> x1, local copies, waits for them, and re-layouts: none -> 2.55 us  [per_device(): jnp.stack([updated] * lax.axis_size('shard'))]
    unnamed x12 -> x8, local copies, waits for them, and re-layouts: 4.74 us -> 6.72 us
  transfers between devices with their start and end apart: 1 -> 1, of which waited for: 1 -> 1; matrix products, arithmetic and copies ran while one was open for 6% -> 7% of each run, Pallas kernels for 0% -> 0%
where the time goes in v1:
time: 183 us; the launch traced here: 182 us
  blocking collectives  61.4 us (34%)
  local copies, waits for them, and re-layouts  39.3 us (21%)
  waiting for transfers between devices  35.2 us (19%)
  other arithmetic  22.2 us (12%)
  matrix products  17.5 us (10%)
  starting transfers between devices  5.51 us (3%)
    all_to_all x1, waiting for transfers between devices, per_device(): lax.all_to_all(jnp.stack([updated] * lax.axis_size('shard')), 'shard', 0, 0)  35.2 us
    all_to_all x2, blocking collectives, copy_for_each(): return lax.all_to_all(copies, axis, split_axis=0, concat_axis=0, tiled=True)  28.6 us
    all_to_all x1, blocking collectives, sum_in_two_steps(): lax.all_to_all(nearer, far, split_axis=0, concat_axis=0, tiled=True)  24.6 us
    unnamed x4, other arithmetic  13.7 us
    all_to_all x1, blocking collectives, sent_and_summed(): blocks = lax.all_to_all(in_blocks(array, dim, size), axis, 0, 0, tiled=True)  8.23 us
    unnamed x8, local copies, waits for them, and re-layouts  6.72 us
    dot_general x2, matrix products, decode(): jnp.einsum('ai,xyab,bj->xiyj', basis_table, square, basis_table, precisio...  6.7 us
    all_to_all x1, local copies, waits for them, and re-layouts, per_device(): lax.all_to_all(jnp.stack([updated] * lax.axis_size('shard')), 'shard', 0, 0)  6.45 us
  transfers between devices with their start and end apart: 1, of which 1 were waited for; matrix products, arithmetic and copies ran while one was open for 7% of the time, Pallas kernels for 0%

profile of v1, /device:TPU:1, one launch (start us, length us, event | category | flops | bytes accessed | tf_op | source)
XLA Modules:
  0.0 181.9 jit_solution(1802421718927631392)
XLA Ops:
  0.6 0.8 compare_select_fusion
  1.4 0.8 add_select_fusion
  3.8 0.8 fusion.11
  4.6 0.8 fusion.10
  5.6 1.9 %add.62 = f32[4,64,16,64]{3,2,1,0:T(8,128)} reshape(f32[1,256,1024]{2,1,0:T(8,128)S(1)} %convert_add_fusion) | data formatting | bytes 2097152 | tf_op jit(solution)/shard_map/add | solution.py:115
  7.4 4.2 %fusion.5 = f32[4,16,32]{2,1,0:T(8,128)S(1)} fusion(f32[4,16,32,64]{3,2,1,0:T(8,128)S(1)} %fusion.11, f32[4,16,32,64]{3,2,1,0:T(8,128)S(1)} %fusion.10, f32[4,64,16,64]{3,2,1,0:T(8,128)} %add.62), kind=kOutput, calls=%fused_computation.7 | convolution fusion | flops 100923392 | bytes 2105344 | tf_op jit(solution)/shard_map/xyki,xiyj->xykj/dot_general | solution.py:79
  11.7 12.2 %scatter_custom_fusion = f32[262144]{0:T(1024)} fusion(s32[2048]{0:T(1024)S(1)} %reshape.137, f32[2048]{0:T(1024)S(1)} %reshape.139, f32[]{:T(128)} %constant.54.clone.1), kind=kCustom, calls=%fused_computation.16 | custom fusion | flops 2048 | bytes 1048580
  23.9 2.7 %reshape_reshape.3 = f32[16,2,2,4096]{3,2,1,0:T(2,128)} reshape(f32[262144]{0:T(1024)} %scatter_custom_fusion) | data formatting | bytes 2097152 | tf_op jit(solution)/shard_map/reshape;reshape | solution.py:38
  26.7 1.3 copy.41
  28.0 8.2 %all_to_all.25 = f32[2,16,2,4096]{3,2,1,0:T(2,128)} all-to-all(f32[2,16,2,4096]{3,2,1,0:T(2,128)S(1)} %copy.41), channel_id=1, replica_groups=mesh['replica_0'=4,'replica_1'=4,'replica_2'=2,'shard'=8] {'replica_2'}, dimensions={0} | all-to-all | bytes 2097152 | tf_op jit(solution)/shard_map/all_to_all | solution.py:43
  36.2 2.9 %reduce_sum.28 = f32[16,2,4096]{2,1,0:T(2,128)} reduce(f32[2,16,2,4096]{3,2,1,0:T(2,128)} %all_to_all.25, f32[]{:T(128)} %constant.54.clone.1), dimensions={0}, to_apply=%region_2.3 | reduce | flops 131072 | bytes 1572868 | tf_op jit(solution)/shard_map/reduce_sum | solution.py:44
  39.1 24.6 %all_to_all.26 = f32[16,2,4096]{2,1,0:T(2,128)} all-to-all(f32[16,2,4096]{2,1,0:T(2,128)} %reduce_sum.28), channel_id=1, replica_groups=mesh['replica_0'=4,'replica_1'=4,'replica_2'=2,'shard'=8] {'replica_0','..., dimensions={0} | all-to-all | bytes 1048576 | tf_op jit(solution)/shard_map/all_to_all | solution.py:51
  63.7 1.2 reduce_sum.29
  65.1 20.8 %all_to_all.27 = f32[16,2,4096]{2,1,0:T(2,128)S(1)} all-to-all(f32[16,2,4096]{2,1,0:T(2,128)S(1)} %broadcast_in_dim.23), channel_id=1, replica_groups=mesh['replica_0'=4,'replica_1'=4,'replica_2'=2,'shard'=8] {'replica_0','..., dimensions={0} | all-to-all | bytes 1048576 | tf_op jit(solution)/shard_map/all_to_all | solution.py:21
  86.6 7.7 %all_to_all.28 = f32[2,16,2,4096]{3,2,1,0:T(2,128)S(1)} all-to-all(f32[2,16,2,4096]{3,2,1,0:T(2,128)S(1)} %broadcast_in_dim.24), channel_id=1, replica_groups=mesh['replica_0'=4,'replica_1'=4,'replica_2'=2,'shard'=8] {'replica_2'}, dimensions={0} | all-to-all | bytes 2097152 | tf_op jit(solution)/shard_map/all_to_all | solution.py:21
  94.3 1.0 copy.43
  95.4 3.2 %reshape_reshape_reshape_reshape.3 = f32[4,16,64,64]{3,2,1,0:T(8,128)} reshape(f32[16,2,2,4096]{3,2,1,0:T(2,128)} %copy.43) | data formatting | bytes 2097152 | tf_op jit(solution)/shard_map/reshape;reshape;reshape;reshape | solution.py:105
  98.5 3.6 %fusion.19 = f32[4,16,64,64]{2,3,1,0:T(8,128)S(1)} fusion(f32[4,16,64,64]{3,2,1,0:T(8,128)} %reshape_reshape_reshape_reshape.3, f32[64]{0:T(128)S(1)} %get-tuple-element.17, f32[64]{0:T(128)S(1)} %get-tuple-element.16), kind=kOutput, calls=%fused_computation.32 | convolution fusion | flops 201338880 | bytes 2097664 | tf_op jit(solution)/shard_map/ai,xyab,bj->xiyj/dot_general | solution.py:106
  102.2 3.1 %multiply_bitcast_fusion = (f32[4,64,16,64]{3,1,2,0:T(8,128)S(1)}, bf16[4,64,16,64]{3,1,2,0:T(8,128)(2,1)}) fusion(f32[4,16,64,64]{2,3,1,0:T(8,128)S(1)} %fusion.19, f32[64]{0:T(128)S(1)} %get-tuple-element.17, f32[64]{0:T(128)S(1)} %get-tuple-element.16), kind=kOutput, calls=%fused_computation.3 | convolution fusion | flops 201863168 | bytes 2621952 | tf_op jit(solution)/shard_map/ai,xyab,bj->xiyj/dot_general | solution.py:106
  105.2 2.5 %copy.47 = f32[4,64,16,64]{3,2,1,0:T(8,128)} copy(f32[4,64,16,64]{3,1,2,0:T(8,128)S(1)} %get-tuple-element.12) | data formatting | bytes 2097152 | tf_op jit(solution)/shard_map/mul | solution.py:120
  107.8 2.7 %mul.124 = f32[256,1024]{1,0:T(8,128)} reshape(f32[4,64,16,64]{3,2,1,0:T(8,128)} %copy.47) | data formatting | bytes 2097152 | tf_op jit(solution)/shard_map/mul | solution.py:120
  110.5 1.5 subtract_convert_fusion
  112.0 2.6 %stack.2 = bf16[8,256,1024]{2,1,0:T(8,128)(2,1)} broadcast(bf16[256,1024]{1,0:T(8,128)(2,1)S(1)} %subtract_convert_fusion), dimensions={1,2} | broadcast | bytes 4718592 | tf_op jit(solution)/shard_map/stack | solution.py:122
  114.6 5.5 %all-to-all-start.4 = ((bf16[8,256,1024]{2,1,0:T(8,128)(2,1)}), bf16[8,256,1024]{2,1,0:T(8,128)(2,1)}, u32[]{:S(2)}, u32[]{:S(2)}) async-start(bf16[8,256,1024]{2,1,0:T(8,128)(2,1)} %stack.2), calls=%async_computation.4 | async-start | bytes 8388608 | tf_op jit(solution)/shard_map/all_to_all | solution.py:122
  120.1 5.1 %convolution_bitcast_fusion = f32[4,64,16,64]{1,3,2,0:T(8,128)} fusion(f32[4,16,32,64]{3,2,1,0:T(8,128)S(1)} %fusion.10, f32[4,16,32,64]{3,2,1,0:T(8,128)S(1)} %fusion.11, f32[4,16,32]{2,1,0:T(8,128)S(1)} %fusion.5), kind=kOutput, calls=%fused_computation.5 | convolution fusion | flops 100794368 | bytes 2105344 | tf_op jit(solution)/shard_map/xyki,xyk,xykj->xiyj/dot_general | solution.py:89
  125.2 3.1 %copy.40 = f32[4,64,16,64]{3,2,1,0:T(8,128)} copy(f32[4,64,16,64]{1,3,2,0:T(8,128)} %convolution_bitcast_fusion) | data formatting | bytes 2097152 | tf_op jit(solution)/shard_map/xyki,xyk,xykj->xiyj/transpose | solution.py:89
  128.2 2.0 %reshape.129 = f32[1,256,1024]{2,1,0:T(8,128)S(1)} reshape(f32[4,64,16,64]{3,2,1,0:T(8,128)} %copy.40) | data formatting | bytes 2097152 | tf_op jit(solution)/shard_map/reshape | solution.py:92
  130.3 1.2 sub.16
  132.4 1.5 convert_element_type.28
  133.9 35.2 %all-to-all-done.4 = bf16[8,256,1024]{2,1,0:T(8,128)(2,1)} async-done(((bf16[8,256,1024]{2,1,0:T(8,128)(2,1)}), bf16[8,256,1024]{2,1,0:T(8,128)(2,1)}, u32[]{:S(2)}, u32[]{:S(2)}) %all-to-all-start.4) | async-done | bytes 4194336 | tf_op jit(solution)/shard_map/all_to_all | solution.py:122
  169.1 6.4 %copy.48 = bf16[8,256,1024]{1,2,0:T(8,128)(2,1)} copy(bf16[8,256,1024]{2,1,0:T(8,128)(2,1)} %all-to-all-done.4) | data formatting | bytes 8388608 | tf_op jit(solution)/shard_map/all_to_all | solution.py:122
  175.6 6.3 %copy.49 = bf16[256,8192]{1,0:T(8,128)(2,1)} copy(bf16[256,8192]{0,1:T(8,128)(2,1)} %bitcast.62) | data formatting | bytes 8388608
  (18 shorter events, 3.6 us)
Async XLA Ops:
  3.8 1.6 copy-start.1
  3.8 1.6 copy-start.2
  114.6 54.6 %all-to-all-start.4 = ((bf16[8,256,1024]{2,1,0:T(8,128)(2,1)}), bf16[8,256,1024]{2,1,0:T(8,128)(2,1)}, u32[]{:S(2)}, u32[]{:S(2)}) async-start(bf16[8,256,1024]{2,1,0:T(8,128)(2,1)} %stack.2), calls=%async_computation.4 | async-start | bytes 8388608 | tf_op jit(solution)/shard_map/all_to_all | solution.py:122
  130.3 1.5 copy-start
